TPU v7x, 32 devices: a whole 2x2x4 slice. The times are simulated.
32 devices in a mesh: dp: 2 (over y), ctx: 4 (over z), fsdp: 4 (over x, core).
Axes of the slice: x: 2, y: 2, z: 4, core: 2. Of those that a mesh axis runs over, the one named last changes fastest.
Arguments:
- inputs: bfloat16 [2, 4096, 640], P('dp', ('ctx', 'fsdp')), may hold values from -6 to 6
- positions: int32 [2, 4096], P('dp', ('ctx', 'fsdp')), may hold values from 0 to 4095, as said below
- cotangent: bfloat16 [2, 4096, 640], P('dp', ('ctx', 'fsdp')), may hold values from -6 to 6
- w_query: bfloat16 [640, 1024], P('fsdp'), may hold values from -0.25 to 0.25
- w_key: bfloat16 [640, 256], P('fsdp'), may hold values from -0.25 to 0.25
- w_value: bfloat16 [640, 256], P('fsdp'), may hold values from -0.25 to 0.25
- w_out: bfloat16 [1024, 640], P('fsdp'), may hold values from -0.375 to 0.375
- w_gate: bfloat16 [640, 2048], P('fsdp'), may hold values from -0.25 to 0.25
- w_up: bfloat16 [640, 2048], P('fsdp'), may hold values from -0.25 to 0.25
- w_down: bfloat16 [2048, 640], P('fsdp'), may hold values from -0.125 to 0.125
- gain_attn_in: bfloat16 [640], P('fsdp'), may hold values from 0.25 to 1.75
- gain_attn_out: bfloat16 [640], P('fsdp'), may hold values from 0.25 to 1.75
- gain_ffn_in: bfloat16 [640], P('fsdp'), may hold values from 0.25 to 1.75
- gain_ffn_out: bfloat16 [640], P('fsdp'), may hold values from 0.25 to 1.75
- gain_query: bfloat16 [256], P('fsdp'), may hold values from 0.25 to 1.75
- gain_key: bfloat16 [256], P('fsdp'), may hold values from 0.25 to 1.75
Outputs:
- outputs: bfloat16 [2, 4096, 640], P('dp', ('ctx', 'fsdp'))
- input_grad: bfloat16 [2, 4096, 640], P('dp', ('ctx', 'fsdp'))
- grad_w_query: float32 [640, 1024], P('fsdp')
- grad_w_key: float32 [640, 256], P('fsdp')
- grad_w_value: float32 [640, 256], P('fsdp')
- grad_w_out: float32 [1024, 640], P('fsdp')
- grad_w_gate: float32 [640, 2048], P('fsdp')
- grad_w_up: float32 [640, 2048], P('fsdp')
- grad_w_down: float32 [2048, 640], P('fsdp')
- grad_gain_attn_in: float32 [640], P('fsdp')
- grad_gain_attn_out: float32 [640], P('fsdp')
- grad_gain_ffn_in: float32 [640], P('fsdp')
- grad_gain_ffn_out: float32 [640], P('fsdp')
- grad_gain_query: float32 [256], P('fsdp')
- grad_gain_key: float32 [256], P('fsdp')
Inputs may be any that keep to these rules, and one draw needn't show every extreme that they name: In each sequence the positions are a permutation of 0 to 4095. Each device's 256 positions are two runs of 128 consecutive positions, the lower first, beginning at c * 128 and at (31 - c) * 128 for some c, each c once per sequence.
All inputs are finite; a program needn't handle non-finite values.
Results may differ from a plain program's by a relative error of at most 0.019.
Values may be sent and summed in bfloat16 or wider, within the bound.
A program may use at most 320 MiB of HBM per device.

v0:
```python
import math

import jax
import jax.numpy as jnp
import numpy as np
from jax import lax
from jax.sharding import PartitionSpec as P

EPSILON = 1e-06
ROPE_BASE = 1000000.0
NEGATIVE = -1e30


def rms_norm(value, gain):
    return value * lax.rsqrt(jnp.mean(value * value, -1, keepdims=True) + EPSILON) * gain


def rms_back(value, gain, grad):
    inverse = lax.rsqrt(jnp.mean(value * value, -1, keepdims=True) + EPSILON)
    normal = value * inverse
    scaled = grad * gain
    gain_grad = jnp.sum((grad * normal).reshape(-1, value.shape[-1]), 0)
    value_grad = inverse * (scaled - normal * jnp.mean(scaled * normal, -1, keepdims=True))
    return (value_grad, gain_grad)


def rope_tables(place, head_dim, length):
    half = head_dim // 2
    frequency = ROPE_BASE ** (-2.0 * np.arange(half) / head_dim)
    coarse = 128.0 * np.arange(length // 128 + 1)[:, None] * frequency[None, :]
    finer = 1.0 * np.arange(128)[:, None] * frequency[None, :]
    upper = place // 128
    lower = place % 128
    cos_upper = jnp.asarray(np.cos(coarse), jnp.float32)[upper]
    sin_upper = jnp.asarray(np.sin(coarse), jnp.float32)[upper]
    cos_lower = jnp.asarray(np.cos(finer), jnp.float32)[lower]
    sin_lower = jnp.asarray(np.sin(finer), jnp.float32)[lower]
    cosine = cos_upper * cos_lower - sin_upper * sin_lower
    sine = sin_upper * cos_lower + cos_upper * sin_lower
    return (cosine, sine)


def rotate(value, cosine, sine):
    half = value.shape[-1] // 2
    first = value[..., :half]
    second = value[..., half:]
    return jnp.concatenate([first * cosine - second * sine, second * cosine + first * sine], -1)


def contract_rows(left, right):
    return lax.dot_general(
        left, right, (((0,), (0,)), ((), ())), preferred_element_type=jnp.float32
    )


def times_transpose(left, right):
    return lax.dot_general(
        left, right, (((1,), (1,)), ((), ())), preferred_element_type=jnp.float32
    )


def block_scores(query_rows, row_places, keys, index, block, scale):
    key_block = lax.dynamic_slice_in_dim(keys, index * block, block, 0)
    scores = times_transpose(query_rows, key_block) * scale
    key_places = index * block + lax.broadcasted_iota(jnp.int32, (1, block), 1)
    return (jnp.where(key_places <= row_places[:, None], scores, NEGATIVE), key_block)


def softmax_totals(query_rows, row_places, keys, count, block, scale):
    rows = query_rows.shape[0]

    def visit(index, carry):
        peak, total = carry
        scores, unused = block_scores(query_rows, row_places, keys, index, block, scale)
        fresh = jnp.maximum(peak, jnp.max(scores, 1))
        total = total * jnp.exp(peak - fresh) + jnp.sum(jnp.exp(scores - fresh[:, None]), 1)
        return (fresh, total)

    start = (jnp.full((rows,), NEGATIVE, jnp.float32), jnp.zeros((rows,), jnp.float32))
    peak, total = lax.fori_loop(0, count, visit, start)
    return peak + jnp.log(total)


def attend_rows(query_rows, row_places, keys, values, count, block, scale, log_total):

    def visit(index, accum):
        scores, unused = block_scores(query_rows, row_places, keys, index, block, scale)
        probs = jnp.exp(scores - log_total[:, None]).astype(jnp.bfloat16)
        value_block = lax.dynamic_slice_in_dim(values, index * block, block, 0)
        return accum + jnp.dot(probs, value_block, preferred_element_type=jnp.float32)

    return lax.fori_loop(0, count, visit, jnp.zeros(query_rows.shape, jnp.float32))


def attend_back(
    query_rows,
    row_places,
    keys,
    values,
    count,
    block,
    scale,
    log_total,
    grad_rows,
    delta,
    key_grads,
    value_grads,
):

    def visit(index, carry):
        query_grad, key_grads, value_grads = carry
        scores, key_block = block_scores(query_rows, row_places, keys, index, block, scale)
        value_block = lax.dynamic_slice_in_dim(values, index * block, block, 0)
        probs = jnp.exp(scores - log_total[:, None])
        prob_grad = times_transpose(grad_rows, value_block)
        score_grad = (probs * (prob_grad - delta[:, None])).astype(jnp.bfloat16)
        query_grad = query_grad + jnp.dot(score_grad, key_block, preferred_element_type=jnp.float32)
        key_part = contract_rows(score_grad, query_rows)
        value_part = contract_rows(probs.astype(jnp.bfloat16), grad_rows)
        old_keys = lax.dynamic_slice_in_dim(key_grads, index * block, block, 0)
        key_grads = lax.dynamic_update_slice_in_dim(
            key_grads, old_keys + key_part, index * block, 0
        )
        old_values = lax.dynamic_slice_in_dim(value_grads, index * block, block, 0)
        value_grads = lax.dynamic_update_slice_in_dim(
            value_grads, old_values + value_part, index * block, 0
        )
        return (query_grad, key_grads, value_grads)

    start = (jnp.zeros(query_rows.shape, jnp.float32), key_grads, value_grads)
    return lax.fori_loop(0, count, visit, start)


def per_device(
    inputs,
    positions,
    cotangent,
    w_query,
    w_key,
    w_value,
    w_out,
    w_gate,
    w_up,
    w_down,
    gain_attn_in,
    gain_attn_out,
    gain_ffn_in,
    gain_ffn_out,
    gain_query,
    gain_key,
):
    gathered = (
        lax.all_gather(w_query, "fsdp", axis=0, tiled=True),
        lax.all_gather(w_key, "fsdp", axis=0, tiled=True),
        lax.all_gather(w_value, "fsdp", axis=0, tiled=True),
        lax.all_gather(w_out, "fsdp", axis=0, tiled=True),
        lax.all_gather(w_gate, "fsdp", axis=0, tiled=True),
        lax.all_gather(w_up, "fsdp", axis=0, tiled=True),
        lax.all_gather(w_down, "fsdp", axis=0, tiled=True),
        lax.all_gather(gain_attn_in, "fsdp", axis=0, tiled=True),
        lax.all_gather(gain_attn_out, "fsdp", axis=0, tiled=True),
        lax.all_gather(gain_ffn_in, "fsdp", axis=0, tiled=True),
        lax.all_gather(gain_ffn_out, "fsdp", axis=0, tiled=True),
        lax.all_gather(gain_query, "fsdp", axis=0, tiled=True),
        lax.all_gather(gain_key, "fsdp", axis=0, tiled=True),
    )
    query_full, key_full, value_full, out_full, gate_full, up_full, down_full = gathered[:7]
    norm_attn_in, norm_attn_out, norm_ffn_in, norm_ffn_out, norm_query, norm_key = [
        item.astype(jnp.float32) for item in gathered[7:]
    ]
    tokens = inputs.shape[1]
    run_length = tokens // 2
    length = tokens * lax.axis_size("ctx") * lax.axis_size("fsdp")
    head_dim = key_full.shape[1]
    heads = query_full.shape[1] // head_dim
    block = math.gcd(2048, length)
    scale = head_dim ** (-0.5)
    state = inputs[0].astype(jnp.float32)
    place = positions[0]
    outer_grad = cotangent[0].astype(jnp.float32)
    cosine, sine = rope_tables(place, head_dim, length)
    attn_in = rms_norm(state, norm_attn_in).astype(jnp.bfloat16)
    query_proj = jnp.dot(attn_in, query_full, preferred_element_type=jnp.float32).reshape(
        tokens, heads, head_dim
    )
    key_proj = jnp.dot(attn_in, key_full, preferred_element_type=jnp.float32)
    value_proj = jnp.dot(attn_in, value_full, preferred_element_type=jnp.float32)
    queries = rotate(rms_norm(query_proj, norm_query), cosine[:, None, :], sine[:, None, :]).astype(
        jnp.bfloat16
    )
    keys_local = rotate(rms_norm(key_proj, norm_key), cosine, sine).astype(jnp.bfloat16)
    values_local = value_proj.astype(jnp.bfloat16)
    run_places = place.reshape(2, run_length)
    every_start = lax.all_gather(run_places[:, 0], ("ctx", "fsdp"), axis=0, tiled=True)
    run_ids = every_start // run_length
    order = jnp.argsort(run_ids)
    pair = (
        lax.all_gather(keys_local, ("ctx", "fsdp"), axis=0, tiled=True),
        lax.all_gather(values_local, ("ctx", "fsdp"), axis=0, tiled=True),
    )
    all_keys, all_values = tuple(
        (
            jnp.take(item.reshape(-1, run_length, head_dim), order, axis=0).reshape(
                length, head_dim
            )
            for item in pair
        )
    )
    query_runs = queries.reshape(2, run_length * heads, head_dim)
    row_places = jnp.repeat(run_places, heads, axis=1)
    counts = run_places[:, -1] // block + 1
    log_totals = []
    out_runs = []
    for run in range(2):
        log_total = softmax_totals(
            query_runs[run], row_places[run], all_keys, counts[run], block, scale
        )
        log_totals.append(log_total)
        out_runs.append(
            attend_rows(
                query_runs[run],
                row_places[run],
                all_keys,
                all_values,
                counts[run],
                block,
                scale,
                log_total,
            )
        )
    attended = jnp.concatenate(out_runs, 0).reshape(tokens, heads * head_dim).astype(jnp.bfloat16)
    attn_out = jnp.dot(attended, out_full, preferred_element_type=jnp.float32)
    middle = state + rms_norm(attn_out, norm_attn_out)
    ffn_in = rms_norm(middle, norm_ffn_in).astype(jnp.bfloat16)
    gate = jnp.dot(ffn_in, gate_full, preferred_element_type=jnp.float32)
    up_proj = jnp.dot(ffn_in, up_full, preferred_element_type=jnp.float32)
    hidden = (jax.nn.gelu(gate, approximate=True) * up_proj).astype(jnp.bfloat16)
    down = jnp.dot(hidden, down_full, preferred_element_type=jnp.float32)
    result = (middle + rms_norm(down, norm_ffn_out)).astype(jnp.bfloat16)
    again = (
        lax.all_gather(w_query, "fsdp", axis=0, tiled=True),
        lax.all_gather(w_key, "fsdp", axis=0, tiled=True),
        lax.all_gather(w_value, "fsdp", axis=0, tiled=True),
        lax.all_gather(w_out, "fsdp", axis=0, tiled=True),
        lax.all_gather(w_gate, "fsdp", axis=0, tiled=True),
        lax.all_gather(w_up, "fsdp", axis=0, tiled=True),
        lax.all_gather(w_down, "fsdp", axis=0, tiled=True),
    )
    query_full, key_full, value_full, out_full, gate_full, up_full, down_full = again
    down_grad, gain_ffn_out_grad = rms_back(down, norm_ffn_out, outer_grad)
    down_narrow = down_grad.astype(jnp.bfloat16)
    grad_down_w = contract_rows(hidden, down_narrow)
    hidden_grad = times_transpose(down_narrow, down_full)
    unused, pull = jax.vjp(
        lambda left, right: jax.nn.gelu(left, approximate=True) * right, gate, up_proj
    )
    gate_grad, up_grad = pull(hidden_grad)
    gate_narrow = gate_grad.astype(jnp.bfloat16)
    up_narrow = up_grad.astype(jnp.bfloat16)
    grad_gate_w = contract_rows(ffn_in, gate_narrow)
    grad_up_w = contract_rows(ffn_in, up_narrow)
    ffn_in_grad = times_transpose(gate_narrow, gate_full) + times_transpose(up_narrow, up_full)
    middle_part, gain_ffn_in_grad = rms_back(middle, norm_ffn_in, ffn_in_grad)
    middle_grad = outer_grad + middle_part
    attn_grad, gain_attn_out_grad = rms_back(attn_out, norm_attn_out, middle_grad)
    attn_narrow = attn_grad.astype(jnp.bfloat16)
    grad_out_w = contract_rows(attended, attn_narrow)
    attended_grad = times_transpose(attn_narrow, out_full).astype(jnp.bfloat16)
    back_keys, back_values = (all_keys, all_values)
    grad_runs = attended_grad.reshape(2, run_length * heads, head_dim)
    key_grads = jnp.zeros((length, head_dim), jnp.float32)
    value_grads = jnp.zeros((length, head_dim), jnp.float32)
    query_grads = []
    for run in range(2):
        delta = jnp.sum(grad_runs[run].astype(jnp.float32) * out_runs[run], 1)
        query_grad, key_grads, value_grads = attend_back(
            query_runs[run],
            row_places[run],
            back_keys,
            back_values,
            counts[run],
            block,
            scale,
            log_totals[run],
            grad_runs[run],
            delta,
            key_grads,
            value_grads,
        )
        query_grads.append(query_grad * scale)
    key_storage = jnp.take(
        (key_grads * scale).reshape(-1, run_length, head_dim), run_ids, axis=0
    ).reshape(length, head_dim)
    value_storage = jnp.take(
        value_grads.reshape(-1, run_length, head_dim), run_ids, axis=0
    ).reshape(length, head_dim)
    key_local_grad, value_local_grad = (
        lax.psum_scatter(key_storage, ("ctx", "fsdp"), scatter_dimension=0, tiled=True),
        lax.psum_scatter(value_storage, ("ctx", "fsdp"), scatter_dimension=0, tiled=True),
    )
    queries_grad = jnp.concatenate(query_grads, 0).reshape(tokens, heads, head_dim)
    query_proj_grad, gain_query_grad = rms_back(
        query_proj, norm_query, rotate(queries_grad, cosine[:, None, :], -sine[:, None, :])
    )
    key_proj_grad, gain_key_grad = rms_back(
        key_proj, norm_key, rotate(key_local_grad, cosine, -sine)
    )
    query_narrow = query_proj_grad.reshape(tokens, heads * head_dim).astype(jnp.bfloat16)
    key_narrow = key_proj_grad.astype(jnp.bfloat16)
    value_narrow = value_local_grad.astype(jnp.bfloat16)
    grad_query_w = contract_rows(attn_in, query_narrow)
    grad_key_w = contract_rows(attn_in, key_narrow)
    grad_value_w = contract_rows(attn_in, value_narrow)
    attn_in_grad = (
        times_transpose(query_narrow, query_full)
        + times_transpose(key_narrow, key_full)
        + times_transpose(value_narrow, value_full)
    )
    state_part, gain_attn_in_grad = rms_back(state, norm_attn_in, attn_in_grad)
    input_grad = (middle_grad + state_part).astype(jnp.bfloat16)
    shard_sums = (
        lax.psum_scatter(
            grad_query_w.astype(jnp.bfloat16), "fsdp", scatter_dimension=0, tiled=True
        ).astype(jnp.float32),
        lax.psum_scatter(
            grad_key_w.astype(jnp.bfloat16), "fsdp", scatter_dimension=0, tiled=True
        ).astype(jnp.float32),
        lax.psum_scatter(
            grad_value_w.astype(jnp.bfloat16), "fsdp", scatter_dimension=0, tiled=True
        ).astype(jnp.float32),
        lax.psum_scatter(
            grad_out_w.astype(jnp.bfloat16), "fsdp", scatter_dimension=0, tiled=True
        ).astype(jnp.float32),
        lax.psum_scatter(
            grad_gate_w.astype(jnp.bfloat16), "fsdp", scatter_dimension=0, tiled=True
        ).astype(jnp.float32),
        lax.psum_scatter(
            grad_up_w.astype(jnp.bfloat16), "fsdp", scatter_dimension=0, tiled=True
        ).astype(jnp.float32),
        lax.psum_scatter(
            grad_down_w.astype(jnp.bfloat16), "fsdp", scatter_dimension=0, tiled=True
        ).astype(jnp.float32),
        lax.psum_scatter(
            gain_attn_in_grad.astype(jnp.bfloat16), "fsdp", scatter_dimension=0, tiled=True
        ).astype(jnp.float32),
        lax.psum_scatter(
            gain_attn_out_grad.astype(jnp.bfloat16), "fsdp", scatter_dimension=0, tiled=True
        ).astype(jnp.float32),
        lax.psum_scatter(
            gain_ffn_in_grad.astype(jnp.bfloat16), "fsdp", scatter_dimension=0, tiled=True
        ).astype(jnp.float32),
        lax.psum_scatter(
            gain_ffn_out_grad.astype(jnp.bfloat16), "fsdp", scatter_dimension=0, tiled=True
        ).astype(jnp.float32),
        lax.psum_scatter(
            gain_query_grad.astype(jnp.bfloat16), "fsdp", scatter_dimension=0, tiled=True
        ).astype(jnp.float32),
        lax.psum_scatter(
            gain_key_grad.astype(jnp.bfloat16), "fsdp", scatter_dimension=0, tiled=True
        ).astype(jnp.float32),
    )
    totals = lax.psum(
        (
            shard_sums[0],
            shard_sums[1],
            shard_sums[2],
            shard_sums[3],
            shard_sums[4],
            shard_sums[5],
            shard_sums[6],
            shard_sums[7],
            shard_sums[8],
            shard_sums[9],
            shard_sums[10],
            shard_sums[11],
            shard_sums[12],
        ),
        ("dp", "ctx"),
    )
    return (
        result[None],
        input_grad[None],
        totals[0],
        totals[1],
        totals[2],
        totals[3],
        totals[4],
        totals[5],
        totals[6],
        totals[7],
        totals[8],
        totals[9],
        totals[10],
        totals[11],
        totals[12],
    )


def solution(mesh):
    in_specs = (
        P("dp", ("ctx", "fsdp"), None),
        P("dp", ("ctx", "fsdp")),
        P("dp", ("ctx", "fsdp"), None),
        P("fsdp", None),
        P("fsdp", None),
        P("fsdp", None),
        P("fsdp", None),
        P("fsdp", None),
        P("fsdp", None),
        P("fsdp", None),
        P("fsdp"),
        P("fsdp"),
        P("fsdp"),
        P("fsdp"),
        P("fsdp"),
        P("fsdp"),
    )
    out_specs = (
        P("dp", ("ctx", "fsdp"), None),
        P("dp", ("ctx", "fsdp"), None),
        P("fsdp", None),
        P("fsdp", None),
        P("fsdp", None),
        P("fsdp", None),
        P("fsdp", None),
        P("fsdp", None),
        P("fsdp", None),
        P("fsdp"),
        P("fsdp"),
        P("fsdp"),
        P("fsdp"),
        P("fsdp"),
        P("fsdp"),
    )
    return jax.shard_map(
        per_device, mesh=mesh, in_specs=in_specs, out_specs=out_specs, check_vma=False
    )
```

profile of v0, /device:TPU:0, one launch (start us, length us, event | category | flops | bytes accessed | tf_op | source)
XLA Modules:
  0.0 885.6 jit_solution(8158964414102938925)
XLA Ops:
  15.7 9.0 %all-reduce.15 = (bf16[640]{0:T(1024)(128)(2,1)S(1)}, bf16[256]{0:T(256)(128)(2,1)S(1)}, bf16[256]{0:T(256)(128)(2,1)S(1)}, bf16[640]{0:T(1024)(128)(2,1)S(1)}, ...) all-reduce(bf16[640]{0:T(1024)(128)(2,1)S(1)} %dynamic-update-slice, ...), channel_id=1, replica_groups=mesh['dp'=2,'ctx'=4,'fsdp'=4] {'fsdp'}, use_global_device_ids=true, to_apply=%add | all-reduce | flops 3072 | bytes 12288
  24.7 7.1 all_gather.56
  33.2 1.5 gather_fusion
  39.7 6.2 all_gather.62
  51.0 11.4 %all-reduce.2 = s32[32]{0:T(128)S(1)} all-reduce(s32[32]{0:T(128)S(1)} %bitcast_dynamic-update-slice_fusion), channel_id=2, replica_groups=mesh['dp'=2,'ctx'=4,'fsdp'=4] {'ctx','fsdp'}, use_global_device_ids=true, to_apply=%add.2 | all-reduce | flops 32 | bytes 256 | tf_op jit(solution)/shard_map/all_gather | solution.py:194
  62.9 1.6 sort.17
  65.4 1.7 copy.75
  69.8 11.7 %all-gather.9.cloned.1.call-done = bf16[4096,256]{0,1:T(8,128)(2,1)} async-done(((bf16[256,256]{0,1:T(8,128)(2,1)}), bf16[4096,256]{0,1:T(8,128)(2,1)}) %all-gather.9.cloned.1.call-update) | async-done | bytes 2097168 | tf_op jit(solution)/shard_map/all_gather | solution.py:198
  81.5 3.3 copy.81
  84.8 2.0 gather_fusion.4
  86.8 37.8 %all-gather.13.cloned.1.call-done = bf16[4096,256]{1,0:T(8,128)(2,1)} async-done(((bf16[256,256]{1,0:T(8,128)(2,1)}), bf16[4096,256]{1,0:T(8,128)(2,1)}) %all-gather.13.cloned.1.call-update) | async-done | bytes 2097168 | tf_op jit(solution)/shard_map/all_gather | solution.py:199
  124.6 3.6 gather_fusion.5
  128.2 4.0 broadcast_select_fusion.2
  132.2 3.4 while.78
  136.5 6.0 while.79
  137.3 4.6 fusion.221
  143.6 6.3 while.80
  150.7 11.4 %while.81 = (s32[]{:T(128)}, f32[512,256]{1,0:T(8,128)}, s32[]{:T(128)}, bf16[4096,256]{1,0:T(8,128)(2,1)S(1)}, bf16[512,256]{1,0:T(8,128)(2,1)S(1)}, /*index=5*...) while((s32[]{:T(128)}, f32[512,256]{1,0:T(8,128)}, ...), condition=%wide.region_15.17_spmd.clone, body=%wide.region_14.16_spmd.clone.sunk | while | flops 1079117824 | bytes 3436199 | solution.py:92
  151.5 4.7 fusion.227
  157.0 4.5 fusion.227
  164.2 2.2 convert_element_type.204
  166.3 2.1 multiply_reduce_fusion.9
  170.0 4.1 fusion.123
  174.1 22.9 %all-gather.19.cloned.1.call-done = bf16[640,2048]{1,0:T(8,128)(2,1)} async-done(((bf16[160,2048]{1,0:T(8,128)(2,1)}), bf16[640,2048]{1,0:T(8,128)(2,1)}) %all-gather.19.cloned.1.call-update) | async-done | bytes 2621456 | tf_op jit(solution)/shard_map/all_gather | solution.py:158
  197.0 5.2 multiply_convert_fusion.1
  202.3 21.9 %all-gather.21.cloned.1.call-done = bf16[2048,640]{1,0:T(8,128)(2,1)} async-done(((bf16[512,640]{1,0:T(8,128)(2,1)}), bf16[2048,640]{1,0:T(8,128)(2,1)}) %all-gather.21.cloned.1.call-update) | async-done | bytes 2621456 | tf_op jit(solution)/shard_map/all_gather | solution.py:159
  224.2 3.3 multiply_reduce_fusion.7
  229.2 2.3 multiply_convert_fusion
  232.5 1.5 copy-done.39
  240.5 2.2 broadcast.412
  242.7 2.3 broadcast.412.clone
  245.1 12.0 %while.82 = (s32[]{:T(128)}, f32[512,256]{1,0:T(8,128)S(1)}, f32[4096,256]{1,0:T(8,128)}, f32[4096,256]{1,0:T(8,128)}, s32[]{:T(128)}, /*index=5*/bf16[4096,256]...) while((s32[]{:T(128)}, f32[512,256]{1,0:T(8,128)S(1)}, ...), condition=%wide.region_24.26_spmd.clone, body=%wide.region_23.25_spmd.clone.sunk | while | flops 2693924864 | bytes 108032864 | solution.py:131
  250.8 1.9 copy-done
  253.7 2.0 copy-done.1
  257.2 24.1 %while.83 = (s32[]{:T(128)}, f32[512,256]{1,0:T(8,128)S(1)}, f32[4096,256]{1,0:T(8,128)}, f32[4096,256]{1,0:T(8,128)}, s32[]{:T(128)}, /*index=5*/bf16[4096,256]...) while((s32[]{:T(128)}, f32[512,256]{1,0:T(8,128)S(1)}, ...), condition=%wide.region_27.29_spmd.clone, body=%wide.region_26.28_spmd.clone.sunk | while | flops 2693924864 | bytes 109081472 | solution.py:131
  257.9 2.1 fusion.252
  263.3 1.9 copy-done.2
  266.2 2.0 copy-done.3
  269.7 2.1 fusion.252
  275.1 2.0 copy-done.2
  278.0 2.0 copy-done.3
  283.9 1.7 convolution_convert_fusion.4
  285.7 1.7 convolution_convert_fusion.3
  287.7 3.7 convolution_convert_fusion
  291.6 3.6 convolution_convert_fusion.2
  296.4 2.4 convolution_convert_fusion.1
  299.4 4.4 broadcast_multiply_fusion
  303.8 5.0 gather_fusion.6
  308.9 4.9 gather_fusion.7
  313.8 8.4 broadcast_select_fusion.1
  322.2 5.9 copy.82
  330.2 12.0 %reduce-scatter.20.cloned.1.call-done = bf16[256,640]{1,0:T(8,128)(2,1)} async-done(((bf16[1024,640]{1,0:T(8,128)(2,1)}), bf16[256,640]{1,0:T(8,128)(2,1)}) %reduce-scatter.20.cloned.1.call-update) | async-done | bytes 327696 | tf_op jit(solution)/shard_map/reduce_scatter | solution.py:331
  342.2 37.1 %reduce-scatter.26.cloned.1.call-done = bf16[512,640]{1,0:T(8,128)(2,1)} async-done(((bf16[2048,640]{1,0:T(8,128)(2,1)}), bf16[512,640]{1,0:T(8,128)(2,1)}) %reduce-scatter.26.cloned.1.call-update) | async-done | bytes 655376 | tf_op jit(solution)/shard_map/reduce_scatter | solution.py:340
  379.3 37.4 %reduce-scatter.22.cloned.1.call-done = bf16[160,2048]{1,0:T(8,128)(2,1)} async-done(((bf16[640,2048]{1,0:T(8,128)(2,1)}), bf16[160,2048]{1,0:T(8,128)(2,1)}) %reduce-scatter.22.cloned.1.call-update) | async-done | bytes 655376 | tf_op jit(solution)/shard_map/reduce_scatter | solution.py:334
  416.8 37.1 %reduce-scatter.24.cloned.1.call-done = bf16[160,2048]{1,0:T(8,128)(2,1)} async-done(((bf16[640,2048]{1,0:T(8,128)(2,1)}), bf16[160,2048]{1,0:T(8,128)(2,1)}) %reduce-scatter.24.cloned.1.call-update) | async-done | bytes 655376 | tf_op jit(solution)/shard_map/reduce_scatter | solution.py:337
  453.9 77.2 %reduce-scatter.10.cloned.1.call-done = f32[256,256]{0,1:T(8,128)} async-done(((f32[4096,256]{0,1:T(8,128)}), f32[256,256]{0,1:T(8,128)}) %reduce-scatter.10.cloned.1.call-update) | async-done | bytes 262160 | tf_op jit(solution)/shard_map/reduce_scatter | solution.py:298
  534.7 71.7 %reduce-scatter.12.cloned.1.call-done = f32[256,256]{1,0:T(8,128)} async-done(((f32[4096,256]{1,0:T(8,128)}), f32[256,256]{1,0:T(8,128)}) %reduce-scatter.12.cloned.1.call-update) | async-done | bytes 262160 | tf_op jit(solution)/shard_map/reduce_scatter | solution.py:299
  607.7 2.7 fusion.94
  610.4 6.0 all-reduce.14
  616.7 2.1 convolution_convert_fusion.6
  619.0 2.0 fusion.100
  621.0 8.1 reduce-scatter.16.cloned.1.call-done
  629.1 23.4 %reduce-scatter.18.cloned.1.call-done = bf16[160,256]{1,0:T(8,128)(2,1)} async-done(((bf16[640,256]{1,0:T(8,128)(2,1)}), bf16[160,256]{1,0:T(8,128)(2,1)}) %reduce-scatter.18.cloned.1.call-update) | async-done | bytes 81936 | tf_op jit(solution)/shard_map/reduce_scatter | solution.py:328
  652.5 226.3 %all-reduce.17 = (f32[160,1024]{1,0:T(8,128)}, f32[160,256]{1,0:T(8,128)}, f32[160,256]{1,0:T(8,128)}, f32[256,640]{1,0:T(8,128)}, f32[160,2048]{1,0:T(8,128)}, ...) all-reduce(bf16[160,1024]{1,0:T(8,128)(2,1)S(1)} %copy-done.54, ...), channel_id=1, replica_groups=mesh['dp'=2,'ctx'=4,'fsdp'=4] {'dp','ctx'}, use_global_device_ids=true, to_apply=%region_34.37 | all-reduce | flops 1393408 | bytes 8361984 | tf_op jit(solution)/shard_map/psum | solution.py:362
  (368 shorter events, 71.3 us)
Async XLA Ops:
  7.2 27.6 %copy-start.10 = (f32[33,128]{1,0:T(8,128)S(1)}, f32[33,128]{1,0:T(8,128)}, u32[]{:S(2)}) copy-start(f32[33,128]{1,0:T(8,128)} %constant.207.clone) | copy-start | bytes 50692
  7.2 28.5 %copy-start.14 = (f32[128,128]{1,0:T(8,128)S(1)}, f32[128,128]{1,0:T(8,128)}, u32[]{:S(2)}) copy-start(f32[128,128]{1,0:T(8,128)} %constant.208.clone) | copy-start | bytes 196612
  7.2 29.3 %copy-start.13 = (f32[128,128]{1,0:T(8,128)S(1)}, f32[128,128]{1,0:T(8,128)}, u32[]{:S(2)}) copy-start(f32[128,128]{1,0:T(8,128)} %constant.209.clone) | copy-start | bytes 196612
  7.2 58.1 %all-gather.11.cloned.1.call-start = ((), (), s32[]{:S(2)}) async-start(), calls=%async_computation.10 | async-start | bytes 1638400 | tf_op jit(solution)/shard_map/all_gather | solution.py:153
  8.0 73.6 %all-gather.9.cloned.1.call-start = ((), (), s32[]{:S(2)}) async-start(), calls=%async_computation.9 | async-start | bytes 2228224 | tf_op jit(solution)/shard_map/all_gather | solution.py:198
  24.7 42.4 %copy-start.55 = (f32[640]{0:T(1024)}, f32[640]{0:T(1024)S(1)}, u32[]{:S(2)}) copy-start(f32[640]{0:T(1024)S(1)} %convert_element_type.196) | copy-start | bytes 7684
  31.8 5.8 copy-start.43
  31.8 6.2 copy-start.65
  33.2 4.2 copy-start.15
  37.2 2.5 copy-start.57
  37.5 29.6 %copy-start.61 = (f32[256]{0:T(256)}, f32[256]{0:T(256)S(1)}, u32[]{:S(2)}) copy-start(f32[256]{0:T(256)S(1)} %add_rsqrt_fusion.5) | copy-start | bytes 3076
  38.0 9.5 %copy-start.63 = (f32[256]{0:T(256)}, f32[256]{0:T(256)S(1)}, u32[]{:S(2)}) copy-start(f32[256]{0:T(256)S(1)} %add_rsqrt_fusion.4) | copy-start | bytes 3076
  38.8 30.2 %copy-start.33 = (f32[256,128]{0,1:T(8,128)}, f32[256,128]{0,1:T(8,128)S(1)}, u32[]{:S(2)}) copy-start(f32[256,128]{0,1:T(8,128)S(1)} %get-tuple-element.603) | copy-start | bytes 393220
  38.9 30.1 %copy-start.31 = (f32[256,128]{0,1:T(8,128)}, f32[256,128]{0,1:T(8,128)S(1)}, u32[]{:S(2)}) copy-start(f32[256,128]{0,1:T(8,128)S(1)} %get-tuple-element.610) | copy-start | bytes 393220
  38.9 10.6 %copy-start.73 = (u32[32]{0:T(128)S(1)}, u32[32]{0:T(128)}, u32[]{:S(2)}) copy-start(u32[32]{0:T(128)} %constant.225) | copy-start | bytes 388
  38.9 11.2 %copy-start.60 = (s32[1,256]{1,0:T(1,128)S(1)}, s32[1,256]{1,0:T(1,128)}, u32[]{:S(2)}) copy-start(s32[1,256]{1,0:T(1,128)} %param.37) | copy-start | bytes 3076
  39.6 85.0 %all-gather.13.cloned.1.call-start = ((), (), s32[]{:S(2)}) async-start(), calls=%async_computation.11 | async-start | bytes 2228224 | tf_op jit(solution)/shard_map/all_gather | solution.py:199
  46.0 21.1 %copy-start.45 = (bf16[640,256]{1,0:T(8,128)(2,1)}, bf16[640,256]{1,0:T(8,128)(2,1)S(1)}, u32[]{:S(2)}) copy-start(bf16[640,256]{1,0:T(8,128)(2,1)S(1)} %all_gather.62) | copy-start | bytes 983044
  46.9 119.4 %all-gather.15.cloned.1.call-start = ((), (), s32[]{:S(2)}) async-start(), calls=%async_computation.12 | async-start | bytes 1638400 | tf_op jit(solution)/shard_map/all_gather | solution.py:156
  47.5 122.5 %all-gather.17.cloned.1.call-start = ((), (), s32[]{:S(2)}) async-start(), calls=%async_computation.13 | async-start | bytes 3276800 | tf_op jit(solution)/shard_map/all_gather | solution.py:157
  48.1 148.9 %all-gather.19.cloned.1.call-start = ((), (), s32[]{:S(2)}) async-start(), calls=%async_computation.14 | async-start | bytes 3276800 | tf_op jit(solution)/shard_map/all_gather | solution.py:158
  48.7 175.5 %all-gather.21.cloned.1.call-start = ((), (), s32[]{:S(2)}) async-start(), calls=%async_computation.15 | async-start | bytes 3276800 | tf_op jit(solution)/shard_map/all_gather | solution.py:159
  49.5 280.8 %reduce-scatter.14.cloned.1.call-start = ((), (), s32[]{:S(2)}) async-start(), calls=%async_computation.18 | async-start | bytes 1638400 | tf_op jit(solution)/shard_map/reduce_scatter | solution.py:322
  64.6 3.3 copy-start.67
  162.1 6.3 copy-start.19
  169.4 32.8 %copy-start.21 = (bf16[256,640]{1,0:T(8,128)(2,1)}, bf16[256,640]{1,0:T(8,128)(2,1)S(1)}, u32[]{:S(2)}) copy-start(bf16[256,640]{1,0:T(8,128)(2,1)S(1)} %multiply_convert_fusion.4) | copy-start | bytes 983044
  224.2 3.3 copy-start.35
  224.2 4.6 copy-start.70
  224.2 4.6 copy-start.74
  228.8 2.6 copy-start.47
  229.1 2.3 copy-start.38
  231.4 3.7 copy-start.29
  231.5 3.7 copy-start.49
  231.5 2.5 copy-start.39
  236.5 3.9 copy-start.27
  249.9 2.9 copy-start
  250.8 2.9 copy-start.5
  260.1 2.2 copy-start.20
  262.3 2.9 copy-start.2
  263.3 2.9 copy-start.7
  274.1 2.9 copy-start.2
  275.1 2.9 copy-start.7
  285.7 56.6 %reduce-scatter.20.cloned.1.call-start = ((), (), s32[]{:S(2)}) async-start(), calls=%async_computation.21 | async-start | bytes 1638400 | tf_op jit(solution)/shard_map/reduce_scatter | solution.py:331
  287.5 4.1 copy-start.22
  287.5 91.9 %reduce-scatter.26.cloned.1.call-start = ((), (), s32[]{:S(2)}) async-start(), calls=%async_computation.24 | async-start | bytes 3276800 | tf_op jit(solution)/shard_map/reduce_scatter | solution.py:340
  291.5 125.3 %reduce-scatter.22.cloned.1.call-start = ((), (), s32[]{:S(2)}) async-start(), calls=%async_computation.22 | async-start | bytes 3276800 | tf_op jit(solution)/shard_map/reduce_scatter | solution.py:334
  295.2 158.6 %reduce-scatter.24.cloned.1.call-start = ((), (), s32[]{:S(2)}) async-start(), calls=%async_computation.23 | async-start | bytes 3276800 | tf_op jit(solution)/shard_map/reduce_scatter | solution.py:337
  298.8 232.2 %reduce-scatter.10.cloned.1.call-start = ((), (), s32[]{:S(2)}) async-start(), calls=%async_computation.16 | async-start | bytes 4456448 | tf_op jit(solution)/shard_map/reduce_scatter | solution.py:298
  308.9 4.9 copy-start.69
  328.2 202.9 %copy-start.34 = (f32[256,128]{0,1:T(8,128)S(1)}, f32[256,128]{0,1:T(8,128)}, u32[]{:S(2)}) copy-start(f32[256,128]{0,1:T(8,128)} %copy-done.33) | copy-start | bytes 393220
  328.2 203.9 %copy-start.41 = (f32[256,256]{0,1:T(8,128)S(1)}, f32[256,256]{0,1:T(8,128)}, u32[]{:S(2)}) copy-start(f32[256,256]{0,1:T(8,128)} %copy-done.40) | copy-start | bytes 786436
  328.2 203.9 %copy-start.64 = (f32[256]{0:T(256)S(1)}, f32[256]{0:T(256)}, u32[]{:S(2)}) copy-start(f32[256]{0:T(256)} %copy-done.63) | copy-start | bytes 3076
  328.2 203.9 %copy-start.66 = (f32[256]{0:T(256)S(1)}, f32[256]{0:T(256)}, u32[]{:S(2)}) copy-start(f32[256]{0:T(256)} %copy-done.65) | copy-start | bytes 3076
  328.2 278.2 %reduce-scatter.12.cloned.1.call-start = ((), (), s32[]{:S(2)}) async-start(), calls=%async_computation.17 | async-start | bytes 4456448 | tf_op jit(solution)/shard_map/reduce_scatter | solution.py:299
  328.3 205.2 %copy-start.44 = (bf16[640,256]{1,0:T(8,128)(2,1)S(1)}, bf16[640,256]{1,0:T(8,128)(2,1)}, u32[]{:S(2)}) copy-start(bf16[640,256]{1,0:T(8,128)(2,1)} %copy-done.43) | copy-start | bytes 983044
  328.8 277.6 %copy-start.46 = (bf16[640,256]{1,0:T(8,128)(2,1)S(1)}, bf16[640,256]{1,0:T(8,128)(2,1)}, u32[]{:S(2)}) copy-start(bf16[640,256]{1,0:T(8,128)(2,1)} %copy-done.45) | copy-start | bytes 983044
  328.8 300.3 %reduce-scatter.16.cloned.1.call-start = ((), (), s32[]{:S(2)}) async-start(), calls=%async_computation.19 | async-start | bytes 409600 | tf_op jit(solution)/shard_map/reduce_scatter | solution.py:325
  330.2 277.5 %copy-start.25 = (bf16[640,1024]{1,0:T(8,128)(2,1)S(1)}, bf16[640,1024]{1,0:T(8,128)(2,1)}, u32[]{:S(2)}) copy-start(bf16[640,1024]{1,0:T(8,128)(2,1)} %all-gather.11.cloned.1.call-done) | copy-start | bytes 3932164
  534.7 117.8 %reduce-scatter.18.cloned.1.call-start = ((), (), s32[]{:S(2)}) async-start(), calls=%async_computation.20 | async-start | bytes 409600 | tf_op jit(solution)/shard_map/reduce_scatter | solution.py:328
  607.7 11.3 %copy-start.24 = (f32[256,640]{1,0:T(8,128)S(1)}, f32[256,640]{1,0:T(8,128)}, u32[]{:S(2)}) copy-start(f32[256,640]{1,0:T(8,128)} %copy-done.23) | copy-start | bytes 1966084
  610.4 42.1 %copy-start.50 = (bf16[512,640]{1,0:T(8,128)(2,1)S(1)}, bf16[512,640]{1,0:T(8,128)(2,1)}, u32[]{:S(2)}) copy-start(bf16[512,640]{1,0:T(8,128)(2,1)} %reduce-scatter.26.cloned.1.call-done) | copy-start | bytes 1966084
  610.4 42.1 %copy-start.51 = (bf16[160,2048]{1,0:T(8,128)(2,1)S(1)}, bf16[160,2048]{1,0:T(8,128)(2,1)}, u32[]{:S(2)}) copy-start(bf16[160,2048]{1,0:T(8,128)(2,1)} %reduce-scatter.22.cloned.1.call-done) | copy-start | bytes 1966084
  610.4 42.1 %copy-start.52 = (bf16[160,2048]{1,0:T(8,128)(2,1)S(1)}, bf16[160,2048]{1,0:T(8,128)(2,1)}, u32[]{:S(2)}) copy-start(bf16[160,2048]{1,0:T(8,128)(2,1)} %reduce-scatter.24.cloned.1.call-done) | copy-start | bytes 1966084
  610.4 42.1 %copy-start.54 = (bf16[160,1024]{1,0:T(8,128)(2,1)S(1)}, bf16[160,1024]{1,0:T(8,128)(2,1)}, u32[]{:S(2)}) copy-start(bf16[160,1024]{1,0:T(8,128)(2,1)} %reduce-scatter.14.cloned.1.call-done) | copy-start | bytes 983044
  (33 other events, 51.4 us)
Sparse Core Ops, SparseCore 0:
  9.6 22.3 all-gather.10
  39.8 41.7 all-gather.8
  84.3 40.3 all-gather.12
  126.0 16.9 all-gather.14
  144.4 25.5 all-gather.16
  171.4 25.5 all-gather.18
  198.6 25.5 all-gather.20
  285.8 26.5 reduce-scatter.13
  315.7 26.5 reduce-scatter.19
  344.6 34.6 reduce-scatter.25
  382.0 34.6 reduce-scatter.21
  419.1 34.6 reduce-scatter.23
  458.2 72.7 reduce-scatter.9
  534.8 71.5 reduce-scatter.11
  609.5 19.5 reduce-scatter.15
  632.0 20.4 reduce-scatter.17
where the time goes:
time: 895 us; the launch traced here: 886 us
  waiting for transfers between devices  403 us (45%)
  blocking collectives  266 us (30%)
  local copies, waits for them, and re-layouts  75.2 us (8%)
  matrix products  74.8 us (8%)
  other arithmetic  37.5 us (4%)
  between operations  18.6 us (2%)
  loops' own time  9.89 us (1%)
    psum x1, blocking collectives, per_device(): lax.psum((shard_sums[0], shard_sums[1], shard_sums[2], shard_sums[3], sha...  226 us
    reduce_scatter x1, waiting for transfers between devices, per_device(): lax.psum_scatter(key_storage, ('ctx', 'fsdp'), scatter_dimension=0, tiled...  77.2 us
    reduce_scatter x1, waiting for transfers between devices, per_device(): lax.psum_scatter(value_storage, ('ctx', 'fsdp'), scatter_dimension=0, til...  71.7 us
    all_gather x1, waiting for transfers between devices, per_device(): lax.all_gather(values_local, ('ctx', 'fsdp'), axis=0, tiled=True)  37.8 us
    reduce_scatter x1, waiting for transfers between devices, per_device(): lax.psum_scatter(grad_gate_w.astype(jnp.bfloat16), 'fsdp', scatter_dimens...  37.4 us
    reduce_scatter x1, waiting for transfers between devices, per_device(): lax.psum_scatter(grad_up_w.astype(jnp.bfloat16), 'fsdp', scatter_dimensio...  37.1 us
    reduce_scatter x1, waiting for transfers between devices, per_device(): lax.psum_scatter(grad_down_w.astype(jnp.bfloat16), 'fsdp', scatter_dimens...  37.1 us
    reduce_scatter x1, waiting for transfers between devices, per_device(): lax.psum_scatter(grad_value_w.astype(jnp.bfloat16), 'fsdp', scatter_dimen...  23.4 us
  transfers between devices with their start and end apart: 16, of which 13 were waited for; matrix products, arithmetic and copies ran while one was open for 14% of the time, Pallas kernels for 0%

commit v1 on v0

v1 whole, which is shorter than its diff:
```python
import functools

import jax
import jax.numpy as jnp
import numpy as np
from jax import lax
from jax.experimental import pallas as pl
from jax.experimental.pallas import tpu as pltpu
from jax.sharding import PartitionSpec as P

EPSILON = 1e-06
ROPE_BASE = 1000000.0
VMEM_BYTES = 48 * 1024 * 1024


def rms_norm(value, gain):
    return value * lax.rsqrt(jnp.mean(value * value, -1, keepdims=True) + EPSILON) * gain


def rms_back(value, gain, grad):
    inverse = lax.rsqrt(jnp.mean(value * value, -1, keepdims=True) + EPSILON)
    normal = value * inverse
    scaled = grad * gain
    gain_grad = jnp.sum((grad * normal).reshape(-1, value.shape[-1]), 0)
    value_grad = inverse * (scaled - normal * jnp.mean(scaled * normal, -1, keepdims=True))
    return (value_grad, gain_grad)


def rope_tables(run_ids, run_length, head_dim, length):
    half = head_dim // 2
    frequency = ROPE_BASE ** (-2.0 * np.arange(half) / head_dim)
    coarse = 1.0 * run_length * np.arange(length // run_length + 1)[:, None] * frequency[None, :]
    finer = 1.0 * np.arange(run_length)[:, None] * frequency[None, :]
    cos_upper = jnp.asarray(np.cos(coarse), jnp.float32)[run_ids][:, None, :]
    sin_upper = jnp.asarray(np.sin(coarse), jnp.float32)[run_ids][:, None, :]
    cos_lower = jnp.asarray(np.cos(finer), jnp.float32)[None]
    sin_lower = jnp.asarray(np.sin(finer), jnp.float32)[None]
    cosine = cos_upper * cos_lower - sin_upper * sin_lower
    sine = sin_upper * cos_lower + cos_upper * sin_lower
    return (cosine.reshape(-1, half), sine.reshape(-1, half))


def rotate(value, cosine, sine):
    half = value.shape[-1] // 2
    first = value[..., :half]
    second = value[..., half:]
    return jnp.concatenate([first * cosine - second * sine, second * cosine + first * sine], -1)


def contract_rows(left, right):
    return lax.dot_general(
        left, right, (((0,), (0,)), ((), ())), preferred_element_type=jnp.float32
    )


def times_transpose(left, right):
    return lax.dot_general(
        left, right, (((1,), (1,)), ((), ())), preferred_element_type=jnp.float32
    )


def causal(rows, columns, heads, first):
    token = lax.broadcasted_iota(jnp.int32, (rows, columns), 0) // heads
    key = lax.broadcasted_iota(jnp.int32, (rows, columns), 1) - first
    return key <= token


def forward_kernel(heads, run, ids, mine, query, pair, out, log_total, accum, total):
    step = pl.program_id(0)
    half = run * heads
    width = query.shape[1]

    @pl.when(step == 0)
    def clear():
        accum[...] = jnp.zeros_like(accum)
        total[...] = jnp.zeros_like(total)

    def visit(start, rows, columns, first):
        span = pl.ds(start, rows)
        weights = jnp.exp(times_transpose(query[span, :], pair[:columns, :width]))
        if first is not None:
            weights = jnp.where(causal(rows, columns, heads, first), weights, 0.0)
        folded = weights[:, :run]
        if columns > run:
            folded = folded + weights[:, run:]
        total[span, :] += folded
        accum[span, :] += jnp.dot(
            weights.astype(jnp.bfloat16),
            pair[:columns, width:],
            preferred_element_type=jnp.float32,
        )

    other = ids[step]
    own = mine[0]

    @pl.when(other < own)
    def earlier():
        visit(0, half, run, None)
        visit(half, half, run, None)

    @pl.when(other > own)
    def later():
        visit(half, half, 2 * run, None)

    @pl.when(other == own)
    def diagonal():
        visit(0, half, run, 0)
        visit(half, half, 2 * run, run)

    @pl.when(step == pl.num_programs(0) - 1)
    def finish():
        sums = jnp.sum(total[...], 1, keepdims=True)
        out[...] = accum[...] / sums
        log_total[...] = jnp.broadcast_to(jnp.log(sums), log_total.shape)


def backward_kernel(
    heads, run, ids, mine, query, pair, out_grad, out, log_total, query_grad, pair_grad, delta
):
    step = pl.program_id(0)
    half = run * heads
    width = query.shape[1]

    @pl.when(step == 0)
    def clear():
        query_grad[...] = jnp.zeros_like(query_grad)
        products = out_grad[...].astype(jnp.float32) * out[...]
        delta[...] = jnp.broadcast_to(jnp.sum(products, 1, keepdims=True), delta.shape)

    def visit(start, rows, columns, first):
        span = pl.ds(start, rows)
        keys = pair[:columns, :width]
        repeats = columns // run
        shift = jnp.concatenate([log_total[span, :]] * repeats, 1)
        less = jnp.concatenate([delta[span, :]] * repeats, 1)
        probs = jnp.exp(times_transpose(query[span, :], keys) - shift)
        if first is not None:
            probs = jnp.where(causal(rows, columns, heads, first), probs, 0.0)
        prob_grad = times_transpose(out_grad[span, :], pair[:columns, width:])
        score_grad = (probs * (prob_grad - less)).astype(jnp.bfloat16)
        query_grad[span, :] += jnp.dot(score_grad, keys, preferred_element_type=jnp.float32)
        key_part = contract_rows(score_grad, query[span, :])
        value_part = contract_rows(probs.astype(jnp.bfloat16), out_grad[span, :])
        return (key_part, value_part)

    def store(start, parts):
        rows = parts[0].shape[0]
        pair_grad[start : start + rows, :width] = parts[0].astype(jnp.bfloat16)
        pair_grad[start : start + rows, width:] = parts[1].astype(jnp.bfloat16)

    other = ids[step]
    own = mine[0]

    @pl.when(other < own)
    def earlier():
        store(0, visit(0, 2 * half, run, None))
        pair_grad[run:, :] = jnp.zeros((run, 2 * width), jnp.bfloat16)

    @pl.when(other > own)
    def later():
        store(0, visit(half, half, 2 * run, None))

    @pl.when(other == own)
    def diagonal():
        low = visit(0, half, run, 0)
        high = visit(half, half, 2 * run, run)
        store(0, (high[0][:run] + low[0], high[1][:run] + low[1]))
        store(run, (high[0][run:], high[1][run:]))


def attend(heads, run, ids, mine, query, pairs):
    rows, width = query.shape
    whole = lambda step, *unused: (0, 0)
    return pl.pallas_call(
        functools.partial(forward_kernel, heads, run),
        grid_spec=pltpu.PrefetchScalarGridSpec(
            num_scalar_prefetch=2,
            grid=(ids.shape[0],),
            in_specs=[
                pl.BlockSpec((rows, width), whole),
                pl.BlockSpec((2 * run, 2 * width), lambda step, *unused: (step, 0)),
            ],
            out_specs=[pl.BlockSpec((rows, width), whole), pl.BlockSpec((rows, run), whole)],
            scratch_shapes=[
                pltpu.VMEM((rows, width), jnp.float32),
                pltpu.VMEM((rows, run), jnp.float32),
            ],
        ),
        out_shape=[
            jax.ShapeDtypeStruct((rows, width), jnp.float32),
            jax.ShapeDtypeStruct((rows, run), jnp.float32),
        ],
        compiler_params=pltpu.CompilerParams(vmem_limit_bytes=VMEM_BYTES),
        name="attend",
    )(ids, mine, query, pairs)


def attend_back(heads, run, ids, mine, query, pairs, out_grad, out, log_total):
    rows, width = query.shape
    whole = lambda step, *unused: (0, 0)
    return pl.pallas_call(
        functools.partial(backward_kernel, heads, run),
        grid_spec=pltpu.PrefetchScalarGridSpec(
            num_scalar_prefetch=2,
            grid=(ids.shape[0],),
            in_specs=[
                pl.BlockSpec((rows, width), whole),
                pl.BlockSpec((2 * run, 2 * width), lambda step, *unused: (step, 0)),
                pl.BlockSpec((rows, width), whole),
                pl.BlockSpec((rows, width), whole),
                pl.BlockSpec((rows, run), whole),
            ],
            out_specs=[
                pl.BlockSpec((rows, width), whole),
                pl.BlockSpec((2 * run, 2 * width), lambda step, *unused: (step, 0)),
            ],
            scratch_shapes=[pltpu.VMEM((rows, run), jnp.float32)],
        ),
        out_shape=[
            jax.ShapeDtypeStruct((rows, width), jnp.float32),
            jax.ShapeDtypeStruct(pairs.shape, jnp.bfloat16),
        ],
        compiler_params=pltpu.CompilerParams(vmem_limit_bytes=VMEM_BYTES),
        name="attend_back",
    )(ids, mine, query, pairs, out_grad, out, log_total)


def per_device(
    inputs,
    positions,
    cotangent,
    w_query,
    w_key,
    w_value,
    w_out,
    w_gate,
    w_up,
    w_down,
    gain_attn_in,
    gain_attn_out,
    gain_ffn_in,
    gain_ffn_out,
    gain_query,
    gain_key,
):
    parts = lax.axis_size("fsdp")
    tokens, width = inputs.shape[1:]
    run = tokens // 2
    length = tokens * lax.axis_size("ctx") * parts
    head_dim = w_key.shape[1]
    query_dim = w_query.shape[1]
    heads = query_dim // head_dim
    hidden_dim = w_gate.shape[1]
    scale = head_dim ** (-0.5)

    gains = (gain_attn_in, gain_attn_out, gain_ffn_in, gain_ffn_out, gain_query, gain_key)
    cuts = np.cumsum([0] + [item.shape[0] for item in gains])
    gains_full = lax.all_gather(jnp.concatenate(gains), "fsdp", axis=0, tiled=False)
    qkv_full = lax.all_gather(
        jnp.concatenate([w_query, w_key, w_value], 1), "fsdp", axis=0, tiled=True
    )
    run_ids = positions[0].reshape(2, run)[:, 0] // run
    mine = run_ids[:1]
    ids = lax.all_gather(mine, ("ctx", "fsdp"), axis=0, tiled=True)
    out_full = lax.all_gather(w_out, "fsdp", axis=0, tiled=True)
    gate_up_full = lax.all_gather(
        jnp.concatenate([w_gate, w_up], 1), "fsdp", axis=0, tiled=True
    )
    down_full = lax.all_gather(w_down, "fsdp", axis=0, tiled=True)
    norm_attn_in, norm_attn_out, norm_ffn_in, norm_ffn_out, norm_query, norm_key = [
        gains_full[:, cuts[index] : cuts[index + 1]].reshape(-1).astype(jnp.float32)
        for index in range(len(gains))
    ]

    state = inputs[0].astype(jnp.float32)
    outer_grad = cotangent[0].astype(jnp.float32)
    cosine, sine = rope_tables(run_ids, run, head_dim, length)
    attn_in = rms_norm(state, norm_attn_in).astype(jnp.bfloat16)
    proj = jnp.dot(attn_in, qkv_full, preferred_element_type=jnp.float32)
    query_proj = proj[:, :query_dim].reshape(tokens, heads, head_dim)
    key_proj = proj[:, query_dim : query_dim + head_dim]
    keys = rotate(rms_norm(key_proj, norm_key), cosine, sine).astype(jnp.bfloat16)
    values = proj[:, query_dim + head_dim :].astype(jnp.bfloat16)
    pairs = lax.all_gather(
        jnp.concatenate([keys, values], 1), ("ctx", "fsdp"), axis=0, tiled=True
    )
    queries = rotate(rms_norm(query_proj, norm_query), cosine[:, None, :], sine[:, None, :])
    query_rows = (queries.astype(jnp.bfloat16) * scale).astype(jnp.bfloat16)
    query_rows = query_rows.reshape(tokens * heads, head_dim)
    out_rows, log_total = attend(heads, run, ids, mine, query_rows, pairs)
    attended = out_rows.astype(jnp.bfloat16).reshape(tokens, query_dim)

    attn_out = jnp.dot(attended, out_full, preferred_element_type=jnp.float32)
    middle = state + rms_norm(attn_out, norm_attn_out)
    ffn_in = rms_norm(middle, norm_ffn_in).astype(jnp.bfloat16)
    gate_up = jnp.dot(ffn_in, gate_up_full, preferred_element_type=jnp.float32)
    hidden_of = lambda both: (
        jax.nn.gelu(both[:, :hidden_dim], approximate=True) * both[:, hidden_dim:]
    )
    hidden_wide, pull = jax.vjp(hidden_of, gate_up)
    hidden = hidden_wide.astype(jnp.bfloat16)
    down = jnp.dot(hidden, down_full, preferred_element_type=jnp.float32)
    result = (middle + rms_norm(down, norm_ffn_out)).astype(jnp.bfloat16)

    def shard_sum(grad):
        part = lax.psum_scatter(
            grad.astype(jnp.bfloat16), "fsdp", scatter_dimension=0, tiled=True
        )
        return lax.psum(part, ("dp", "ctx")).astype(jnp.float32)

    down_grad, gain_ffn_out_grad = rms_back(down, norm_ffn_out, outer_grad)
    down_narrow = down_grad.astype(jnp.bfloat16)
    down_sum = shard_sum(contract_rows(hidden, down_narrow))
    gate_up_narrow = pull(times_transpose(down_narrow, down_full))[0].astype(jnp.bfloat16)
    gate_up_sum = shard_sum(contract_rows(ffn_in, gate_up_narrow))
    ffn_in_grad = times_transpose(gate_up_narrow, gate_up_full)
    middle_part, gain_ffn_in_grad = rms_back(middle, norm_ffn_in, ffn_in_grad)
    middle_grad = outer_grad + middle_part
    attn_grad, gain_attn_out_grad = rms_back(attn_out, norm_attn_out, middle_grad)
    attn_narrow = attn_grad.astype(jnp.bfloat16)
    out_sum = shard_sum(contract_rows(attended, attn_narrow))
    attended_grad = times_transpose(attn_narrow, out_full).astype(jnp.bfloat16)
    query_grad, pair_grads = attend_back(
        heads,
        run,
        ids,
        mine,
        query_rows,
        pairs,
        attended_grad.reshape(tokens * heads, head_dim),
        out_rows,
        log_total,
    )
    pair_grad = lax.psum_scatter(
        pair_grads, ("ctx", "fsdp"), scatter_dimension=0, tiled=True
    ).astype(jnp.float32)
    query_proj_grad, gain_query_grad = rms_back(
        query_proj,
        norm_query,
        rotate(
            (query_grad * scale).reshape(tokens, heads, head_dim),
            cosine[:, None, :],
            -sine[:, None, :],
        ),
    )
    key_proj_grad, gain_key_grad = rms_back(
        key_proj, norm_key, rotate(pair_grad[:, :head_dim], cosine, -sine)
    )
    qkv_narrow = jnp.concatenate(
        [
            query_proj_grad.reshape(tokens, query_dim).astype(jnp.bfloat16),
            key_proj_grad.astype(jnp.bfloat16),
            pair_grad[:, head_dim:].astype(jnp.bfloat16),
        ],
        1,
    )
    qkv_sum = shard_sum(contract_rows(attn_in, qkv_narrow))
    attn_in_grad = times_transpose(qkv_narrow, qkv_full)
    state_part, gain_attn_in_grad = rms_back(state, norm_attn_in, attn_in_grad)
    input_grad = (middle_grad + state_part).astype(jnp.bfloat16)
    gain_grads = jnp.concatenate(
        [
            item.reshape(parts, -1)
            for item in (
                gain_attn_in_grad,
                gain_attn_out_grad,
                gain_ffn_in_grad,
                gain_ffn_out_grad,
                gain_query_grad,
                gain_key_grad,
            )
        ],
        1,
    )
    gain_sums = lax.psum(gain_grads, ("dp", "ctx", "fsdp"))
    gain_sum = lax.dynamic_index_in_dim(gain_sums, lax.axis_index("fsdp"), 0, keepdims=False)
    return (
        result[None],
        input_grad[None],
        qkv_sum[:, :query_dim],
        qkv_sum[:, query_dim : query_dim + head_dim],
        qkv_sum[:, query_dim + head_dim :],
        out_sum,
        gate_up_sum[:, :hidden_dim],
        gate_up_sum[:, hidden_dim:],
        down_sum,
        *[gain_sum[cuts[index] : cuts[index + 1]] for index in range(len(gains))],
    )


def solution(mesh):
    in_specs = (
        P("dp", ("ctx", "fsdp"), None),
        P("dp", ("ctx", "fsdp")),
        P("dp", ("ctx", "fsdp"), None),
        P("fsdp", None),
        P("fsdp", None),
        P("fsdp", None),
        P("fsdp", None),
        P("fsdp", None),
        P("fsdp", None),
        P("fsdp", None),
        P("fsdp"),
        P("fsdp"),
        P("fsdp"),
        P("fsdp"),
        P("fsdp"),
        P("fsdp"),
    )
    out_specs = (
        P("dp", ("ctx", "fsdp"), None),
        P("dp", ("ctx", "fsdp"), None),
        P("fsdp", None),
        P("fsdp", None),
        P("fsdp", None),
        P("fsdp", None),
        P("fsdp", None),
        P("fsdp", None),
        P("fsdp", None),
        P("fsdp"),
        P("fsdp"),
        P("fsdp"),
        P("fsdp"),
        P("fsdp"),
        P("fsdp"),
    )
    return jax.shard_map(
        per_device, mesh=mesh, in_specs=in_specs, out_specs=out_specs, check_vma=False
    )
```

time: 895 us -> 579 us (0.65)
  blocking collectives: 266 us -> 60.2 us
  local copies, waits for them, and re-layouts: 75.2 us -> 33.3 us
  matrix products: 74.8 us -> 34.3 us
  Pallas kernels: 0 us -> 32.9 us
  waiting for transfers between devices: 403 us -> 378 us
  other arithmetic: 37.5 us -> 22.9 us
  loops' own time: 9.89 us -> 0 us
    psum x1, blocking collectives: 226 us -> 42.4 us  [per_device(): gain_sums = lax.psum(gain_grads, ('dp', 'ctx', 'fsdp'))]
    reduce_scatter x9 -> x5, waiting for transfers between devices: 304 us -> 200 us  [the longest x4 136 us: shard_sum(): lax.psum_scatter(grad.astype(jnp.bfloat16), 'fsdp', scatter_dimension=0,...]
    psum x0 -> x1, waiting for transfers between devices: none -> 75.5 us  [shard_sum(): return lax.psum(part, ('dp', 'ctx')).astype(jnp.float32)]
    pallas_call x0 -> x2, Pallas kernels: none -> 32.9 us  [the longest x1 18 us: attend_back(): pl.pallas_call(functools.partial(backward_kernel, heads, run), grid_spec=...]
    dot_general x11 -> x2, matrix products: 27.5 us -> 6.71 us  [the longest x1 4.33 us: per_device(): gate_up = jnp.dot(ffn_in, gate_up_full, preferred_element_type=jnp.float32)]
    all_gather x3 -> x1, blocking collectives: 24.7 us -> 6.15 us  [per_device(): lax.all_gather(jnp.concatenate(gains), 'fsdp', axis=0, tiled=False)]
    gather x12 -> x2, local copies, waits for them, and re-layouts: 19.7 us -> 2.58 us  [the longest x1 1.29 us: rope_tables(): sin_upper = jnp.asarray(np.sin(coarse), jnp.float32)[run_ids][:, None, :]]
    while x37 -> x0, local copies, waits for them, and re-layouts: 16.7 us -> none
  transfers between devices with their start and end apart: 16 -> 11, of which waited for: 13 -> 11; matrix products, arithmetic and copies ran while one was open for 14% -> 10% of each run, Pallas kernels for 0% -> 3%
where the time goes in v1:
time: 579 us; the launch traced here: 577 us
  waiting for transfers between devices  378 us (65%)
  blocking collectives  60.2 us (10%)
  matrix products  34.3 us (6%)
  local copies, waits for them, and re-layouts  33.3 us (6%)
  Pallas kernels  32.9 us (6%)
  other arithmetic  22.9 us (4%)
  between operations  14.7 us (3%)
    reduce_scatter x4, waiting for transfers between devices, shard_sum(): lax.psum_scatter(grad.astype(jnp.bfloat16), 'fsdp', scatter_dimension=0,...  136 us
    psum x1, waiting for transfers between devices, shard_sum(): return lax.psum(part, ('dp', 'ctx')).astype(jnp.float32)  75.5 us
    reduce_scatter x1, waiting for transfers between devices, per_device(): lax.psum_scatter(pair_grads, ('ctx', 'fsdp'), scatter_dimension=0, tiled=...  63.7 us
    psum x1, blocking collectives, per_device(): gain_sums = lax.psum(gain_grads, ('dp', 'ctx', 'fsdp'))  42.4 us
    all_gather x1, waiting for transfers between devices, per_device(): lax.all_gather(jnp.concatenate([w_gate, w_up], 1), 'fsdp', axis=0, tiled=...  40.1 us
    all_gather x1, waiting for transfers between devices, per_device(): lax.all_gather(jnp.concatenate([keys, values], 1), ('ctx', 'fsdp'), axis=...  30.9 us
    all_gather x1, waiting for transfers between devices, per_device(): down_full = lax.all_gather(w_down, 'fsdp', axis=0, tiled=True)  18.9 us
    pallas_call x1, Pallas kernels, attend_back(): pl.pallas_call(functools.partial(backward_kernel, heads, run), grid_spec=...  18 us
  transfers between devices with their start and end apart: 11, of which 11 were waited for; matrix products, arithmetic and copies ran while one was open for 10% of the time, Pallas kernels for 3%

profile of v1, /device:TPU:0, one launch (start us, length us, event | category | flops | bytes accessed | tf_op | source)
XLA Modules:
  0.0 577.2 jit_solution(5259913047007443742)
XLA Ops:
  7.2 1.9 pad_maximum_fusion.3
  9.2 4.1 concatenate.45
  13.3 6.1 %all-gather.1 = bf16[4,1,768]{2,1,0:T(2,128)(2,1)S(1)} all-gather(bf16[1,1,768]{2,1,0:T(2,128)(2,1)S(1)} %reshape.347), channel_id=2, replica_groups=mesh['dp'=2,'ctx'=4,'fsdp'=4] {'fsdp'}, dimensions={0}, use_global_device_ids=true | all-gather | bytes 7680 | tf_op jit(solution)/shard_map/all_gather | solution.py:258
  19.5 0.8 copy.39
  20.4 1.3 gather_fusion.1
  21.7 1.3 gather_fusion
  23.2 1.1 fusion.24
  24.3 0.9 multiply_subtract_fusion.2
  25.2 9.5 %all-gather.8.cloned.1.call-done = bf16[640,1536]{1,0:T(8,128)(2,1)} async-done(((bf16[160,1536]{1,0:T(8,128)(2,1)}), bf16[640,1536]{1,0:T(8,128)(2,1)}) %all-gather.8.cloned.1.call-update) | async-done | bytes 1966096 | tf_op jit(solution)/shard_map/all_gather | solution.py:259
  34.8 2.4 fusion.32
  37.9 0.7 pad_maximum_fusion.6
  38.7 0.7 all-gather.12.cloned.1.call-update
  39.5 2.2 pad_maximum_fusion
  43.0 1.2 fusion.43
  44.2 11.7 %all-reduce.2.ids = s32[16]{0:T(128)S(1)} all-reduce(s32[16]{0:T(128)S(1)} %get-tuple-element.74), channel_id=1, replica_groups=mesh['dp'=2,'ctx'=4,'fsdp'=4] {'ctx','fsdp'}, use_global_device_ids=true, to_apply=%add.2 | all-reduce | flops 16 | bytes 128
  56.1 0.7 reshape.325
  58.6 30.9 %all-gather.10.cloned.1.call-done.pair = bf16[4096,512]{1,0:T(8,128)(2,1)} async-done(((bf16[256,512]{1,0:T(8,128)(2,1)}), bf16[4096,512]{1,0:T(8,128)(2,1)}) %all-gather.10.cloned.1.call-update) | async-done | bytes 4194320 | tf_op jit(solution)/shard_map/all_gather | solution.py:284
  89.6 14.9 %attend.1 = (f32[1024,256]{1,0:T(8,128)S(1)}, f32[1024,128]{1,0:T(8,128)S(1)}) custom-call(s32[16]{0:T(128)S(1)} %all-reduce.2.ids, s32[1]{0:T(128)} %get-tuple-element.73.mine, bf16[1024,256]{1,0:T(8,128)(2,1)S(1)} %maximum_multiply_fusion.1.query, bf16[4096,512]{1,0:T(8,128)(2,1)} %all-gather.10.cloned.1.call-done.pair), custom_call_target="tpu_custom_call" | custom-call | tf_op jit(solution)/shard_map/attend/pallas_call | solution.py:174
  104.5 0.8 copy-done
  105.6 2.2 all-gather.12.cloned.1.call-done
  107.9 2.0 multiply_reduce_fusion.8
  110.2 40.1 %all-gather.14.cloned.1.call-done = bf16[640,4096]{1,0:T(8,128)(2,1)} async-done(((bf16[160,4096]{1,0:T(8,128)(2,1)}), bf16[640,4096]{1,0:T(8,128)(2,1)}) %all-gather.14.cloned.1.call-update) | async-done | bytes 5242896 | tf_op jit(solution)/shard_map/all_gather | solution.py:266
  150.3 4.3 fusion.39
  154.7 2.0 copy-done.4
  156.7 1.7 multiply_convert_fusion
  158.4 18.9 %all-gather.16.cloned.1.call-done = bf16[2048,640]{1,0:T(8,128)(2,1)} async-done(((bf16[512,640]{1,0:T(8,128)(2,1)}), bf16[2048,640]{1,0:T(8,128)(2,1)}) %all-gather.16.cloned.1.call-update) | async-done | bytes 2621456 | tf_op jit(solution)/shard_map/all_gather | solution.py:269
  177.3 3.3 multiply_reduce_fusion.6
  180.6 0.9 fusion.25
  181.5 1.0 fusion.16
  182.5 2.3 fusion.13
  184.9 2.4 multiply_reduce_fusion.2
  187.4 1.0 multiply_reduce_fusion.3
  188.6 0.6 copy-done.12
  189.2 0.7 copy-done.26
  190.9 1.0 copy-done.1
  191.9 18.0 %attend_back.1 = (f32[1024,256]{1,0:T(8,128)S(1)}, bf16[4096,512]{1,0:T(8,128)(2,1)}) custom-call(s32[16]{0:T(128)S(1)} %all-reduce.2.ids, s32[1]{0:T(128)} %get-tuple-element.73.mine, bf16[1024,256]{1,0:T(8,128)(2,1)S(1)} %maximum_multiply_fusion.1.query, bf16[4096,512]{1,0:T(8,128)(2,1)} %all-gather.10.cloned.1.call-done.pair, ...), custom_call_target="tpu_custom_call" | custom-call | tf_op jit(solution)/shard_map/attend_back/pallas_call | solution.py:201
  210.0 1.0 copy-done.18
  211.1 1.7 convolution_convert_fusion.3
  212.8 3.5 convolution_convert_fusion.1
  217.6 1.2 copy.40
  219.1 63.7 %reduce-scatter.6.cloned.1.call-done = bf16[256,512]{1,0:T(8,128)(2,1)} async-done(((bf16[4096,512]{1,0:T(8,128)(2,1)}), bf16[256,512]{1,0:T(8,128)(2,1)}) %reduce-scatter.6.cloned.1.call-update) | async-done | bytes 262160 | tf_op jit(solution)/shard_map/reduce_scatter | solution.py:334
  282.9 1.0 convert_element_type.166
  283.9 1.0 multiply_subtract_fusion.1
  284.9 1.2 multiply_subtract_fusion
  286.1 0.9 pad_maximum_fusion.1
  289.9 0.8 copy-done.35
  290.7 2.1 convolution_convert_fusion.2
  292.8 1.0 copy-done.3
  293.9 6.2 %convolution_convert_fusion = bf16[640,4096]{1,0:T(8,128)(2,1)} fusion(f32[256,2048]{1,0:T(8,128)} %copy-done.30, f32[256,2048]{1,0:T(8,128)} %copy-done.29, f32[256,640]{1,0:T(8,128)S(1)} %copy-done.3, f32[640]{0:T(1024)S(1)} %reshape.324, f32[256]{0:T(256)S(1)} %add_rsqrt_fusion.2), kind=kOutput, calls=%fused_computation.2 | convolution fusion | flops 1347387392 | bytes 10096128 | tf_op jit(solution)/shard_map/dot_general | solution.py:51
  300.2 11.6 %reduce-scatter.10.cloned.1.call-done = bf16[256,640]{1,0:T(8,128)(2,1)} async-done(((bf16[1024,640]{1,0:T(8,128)(2,1)}), bf16[256,640]{1,0:T(8,128)(2,1)}) %reduce-scatter.10.cloned.1.call-update) | async-done | bytes 327696 | tf_op jit(solution)/shard_map/reduce_scatter | solution.py:306
  311.7 37.2 %reduce-scatter.14.cloned.1.call-done = bf16[512,640]{1,0:T(8,128)(2,1)} async-done(((bf16[2048,640]{1,0:T(8,128)(2,1)}), bf16[512,640]{1,0:T(8,128)(2,1)}) %reduce-scatter.14.cloned.1.call-update) | async-done | bytes 655376 | tf_op jit(solution)/shard_map/reduce_scatter | solution.py:306
  348.9 33.4 %reduce-scatter.8.cloned.1.call-done = bf16[160,1536]{1,0:T(8,128)(2,1)} async-done(((bf16[640,1536]{1,0:T(8,128)(2,1)}), bf16[160,1536]{1,0:T(8,128)(2,1)}) %reduce-scatter.8.cloned.1.call-update) | async-done | bytes 491536 | tf_op jit(solution)/shard_map/reduce_scatter | solution.py:306
  382.3 53.9 %reduce-scatter.12.cloned.1.call-done = bf16[160,4096]{1,0:T(8,128)(2,1)} async-done(((bf16[640,4096]{1,0:T(8,128)(2,1)}), bf16[160,4096]{1,0:T(8,128)(2,1)}) %reduce-scatter.12.cloned.1.call-update) | async-done | bytes 1310736 | tf_op jit(solution)/shard_map/reduce_scatter | solution.py:306
  436.5 1.0 rsqrt.64
  437.8 3.5 fusion.23
  441.9 42.4 %psum.39 = f32[4,768]{1,0:T(4,128)S(1)} all-reduce(f32[4,768]{1,0:T(4,128)S(1)} %concatenate.59), channel_id=1, replica_groups=mesh['dp'=2,'ctx'=4,'fsdp'=4] {'dp','ctx','fsdp'}, use_global_device_ids=true, to_apply=%region_27.28 | all-reduce | flops 3072 | bytes 24576 | tf_op jit(solution)/shard_map/psum | solution.py:375
  484.9 0.6 fusion.42
  485.5 2.1 fusion.27
  487.6 75.5 %all-reduce.6.cloned.1.call-done = (bf16[160,1536]{1,0:T(8,128)(2,1)}, bf16[256,640]{1,0:T(8,128)(2,1)}, bf16[160,4096]{1,0:T(8,128)(2,1)}, bf16[512,640]{1,0:T(8,128)(2,1)}) async-done(((bf16[160,1536]{1,0:T(8,128)(2,1)}, bf16[256,640]{1,0:T(8,128)(2,1)}, bf16[160,4096]{1,0:T(8,128)(2,1)}, bf16[512,640]{1,0:T(8,128)(2,1)}), (bf16[160,1536]{1,0:T(8,128)(2,1)}, bf16[256,640]{1,0:T(8,128)(2,1)}, ...) | async-done | bytes 2785296 | tf_op jit(solution)/shard_map/psum | solution.py:309
  563.1 2.0 slice.185
  565.1 1.7 fusion.41
  566.8 0.9 convert_element_type.172
  567.7 1.8 fusion.40
  569.5 1.1 convert_element_type.176
  (196 shorter events, 12.8 us)
Async XLA Ops:
  7.2 27.6 %copy-start.14 = (bf16[1,256,640]{2,1,0:T(8,128)(2,1)S(1)}, bf16[1,256,640]{2,1,0:T(8,128)(2,1)}, u32[]{:S(2)}) copy-start(bf16[1,256,640]{2,1,0:T(8,128)(2,1)} %param.20) | copy-start | bytes 983044
  7.2 27.6 %all-gather.8.cloned.1.call-start = ((), (), s32[]{:S(2)}) async-start(), calls=%async_computation.5 | async-start | bytes 2457600 | tf_op jit(solution)/shard_map/all_gather | solution.py:259
  9.2 80.4 %all-gather.10.cloned.1.call-start = ((), (), s32[]{:S(2)}) async-start(), calls=%async_computation.6 | async-start | bytes 4456448 | tf_op jit(solution)/shard_map/all_gather | solution.py:284
  20.4 16.8 %copy-start.39 = (f32[640]{0:T(1024)}, f32[640]{0:T(1024)S(1)}, u32[]{:S(2)}) copy-start(f32[640]{0:T(1024)S(1)} %reshape.320) | copy-start | bytes 7684
  23.2 14.2 %copy-start.44 = (f32[256]{0:T(256)}, f32[256]{0:T(256)S(1)}, u32[]{:S(2)}) copy-start(f32[256]{0:T(256)S(1)} %reshape.322) | copy-start | bytes 3076
  24.3 12.9 %copy-start.52 = (f32[256]{0:T(256)}, f32[256]{0:T(256)S(1)}, u32[]{:S(2)}) copy-start(f32[256]{0:T(256)S(1)} %add_rsqrt_fusion.5) | copy-start | bytes 3076
  25.2 32.9 %copy-start.21 = (f32[2,128,128]{2,1,0:T(8,128)}, f32[2,128,128]{2,1,0:T(8,128)S(1)}, u32[]{:S(2)}) copy-start(f32[2,128,128]{2,1,0:T(8,128)S(1)} %get-tuple-element.58) | copy-start | bytes 393220
  25.2 32.9 %copy-start.28 = (f32[2,128,128]{2,1,0:T(8,128)}, f32[2,128,128]{2,1,0:T(8,128)S(1)}, u32[]{:S(2)}) copy-start(f32[2,128,128]{2,1,0:T(8,128)S(1)} %get-tuple-element.59) | copy-start | bytes 393220
  37.2 19.6 %copy-start.8 = (f32[256,1536]{1,0:T(8,128)}, f32[256,1536]{1,0:T(8,128)S(1)}, u32[]{:S(2)}) copy-start(f32[256,1536]{1,0:T(8,128)S(1)} %fusion.32) | copy-start | bytes 4718596
  37.2 2.3 copy-start.32
  38.7 69.2 %all-gather.12.cloned.1.call-start = ((), (), s32[]{:S(2)}) async-start(), calls=%async_computation.7 | async-start | bytes 1638400 | tf_op jit(solution)/shard_map/all_gather | solution.py:265
  39.4 3.0 copy-start.56
  39.4 110.9 %all-gather.14.cloned.1.call-start = ((), (), s32[]{:S(2)}) async-start(), calls=%async_computation.8 | async-start | bytes 6553600 | tf_op jit(solution)/shard_map/all_gather | solution.py:266
  41.7 135.6 %all-gather.16.cloned.1.call-start = ((), (), s32[]{:S(2)}) async-start(), calls=%async_computation.9 | async-start | bytes 3276800 | tf_op jit(solution)/shard_map/all_gather | solution.py:269
  42.3 240.5 %reduce-scatter.6.cloned.1.call-start = ((), (), s32[]{:S(2)}) async-start(), calls=%async_computation.10 | async-start | bytes 4456448 | tf_op jit(solution)/shard_map/reduce_scatter | solution.py:334
  56.0 1.8 copy-start.42
  56.9 1.3 copy-start.10
  57.4 1.1 copy-start.6
  57.8 0.8 copy-start.22
  105.6 4.2 copy-start.17
  109.9 44.8 %copy-start.48 = (f32[256]{0:T(256)}, f32[256]{0:T(256)S(1)}, u32[]{:S(2)}) copy-start(f32[256]{0:T(256)S(1)} %add_rsqrt_fusion.3) | copy-start | bytes 3076
  110.2 77.2 %copy-start.2 = (f32[256,640]{1,0:T(8,128)}, f32[256,640]{1,0:T(8,128)S(1)}, u32[]{:S(2)}) copy-start(f32[256,640]{1,0:T(8,128)S(1)} %get-tuple-element.39) | copy-start | bytes 1966084
  154.7 2.1 copy-start.4
  158.4 22.2 %copy-start.25 = (bf16[1,256,640]{2,1,0:T(8,128)(2,1)S(1)}, bf16[1,256,640]{2,1,0:T(8,128)(2,1)}, u32[]{:S(2)}) copy-start(bf16[1,256,640]{2,1,0:T(8,128)(2,1)} %param.22) | copy-start | bytes 983044
  177.3 3.3 copy-start.41
  177.3 5.2 copy-start.5
  180.6 1.9 copy-start.55
  181.5 3.3 slice-start
  182.5 2.3 copy-start.31
  182.5 2.4 slice-start.1
  184.8 2.5 copy-start.29
  184.8 2.5 copy-start.30
  184.9 2.5 copy-start.49
  187.3 2.6 copy-start.15
  188.3 0.8 copy-start.12
  190.9 1.0 copy-start.1
  209.9 1.0 copy-start.18
  209.9 1.1 copy-start.27
  210.0 2.9 copy-start.19
  210.0 101.7 %reduce-scatter.10.cloned.1.call-start = ((), (), s32[]{:S(2)}) async-start(), calls=%async_computation.12 | async-start | bytes 1638400 | tf_op jit(solution)/shard_map/reduce_scatter | solution.py:306
  212.8 136.2 %reduce-scatter.14.cloned.1.call-start = ((), (), s32[]{:S(2)}) async-start(), calls=%async_computation.14 | async-start | bytes 3276800 | tf_op jit(solution)/shard_map/reduce_scatter | solution.py:306
  216.3 0.9 copy-start.23
  216.4 166.0 %reduce-scatter.8.cloned.1.call-start = ((), (), s32[]{:S(2)}) async-start(), calls=%async_computation.11 | async-start | bytes 2457600 | tf_op jit(solution)/shard_map/reduce_scatter | solution.py:306
  219.1 67.0 %copy-start.7 = (f32[256,4,256]{2,1,0:T(4,128)S(1)}, f32[256,4,256]{2,1,0:T(4,128)}, u32[]{:S(2)}) copy-start(f32[256,4,256]{2,1,0:T(4,128)} %copy-done.6) | copy-start | bytes 3145732
  282.8 3.3 copy-start.24
  287.4 1.0 copy-start.34
  287.4 1.5 copy-start.9
  287.4 1.5 copy-start.45
  287.4 1.5 copy-start.47
  287.6 1.6 copy-start.20
  288.3 1.4 copy-start.38
  289.2 1.4 copy-start.40
  289.2 1.4 copy-start.53
  292.7 1.1 copy-start.3
  292.8 143.4 %reduce-scatter.12.cloned.1.call-start = ((), (), s32[]{:S(2)}) async-start(), calls=%async_computation.13 | async-start | bytes 6553600 | tf_op jit(solution)/shard_map/reduce_scatter | solution.py:306
  300.1 136.1 %copy-start.11 = (f32[256,1024]{1,0:T(8,128)S(1)}, f32[256,1024]{1,0:T(8,128)}, u32[]{:S(2)}) copy-start(f32[256,1024]{1,0:T(8,128)} %copy-done.10) | copy-start | bytes 3145732
  300.1 263.0 %all-reduce.6.cloned.1.call-start = ((), (), s32[]{:S(2)}) async-start(), calls=%async_computation.15 | async-start | bytes 5570560 | tf_op jit(solution)/shard_map/psum | solution.py:309
  436.2 1.4 copy-start.51
  436.2 1.5 copy-start.54
  436.2 1.5 copy-start.50
  441.3 44.2 %copy-start.13 = (f32[256,640]{1,0:T(8,128)S(1)}, f32[256,640]{1,0:T(8,128)}, u32[]{:S(2)}) copy-start(f32[256,640]{1,0:T(8,128)} %copy-done.12) | copy-start | bytes 1966084
  563.1 3.7 copy-start.36
  563.1 4.6 copy-start.16
  567.7 1.8 copy-start.33
  (6 other events, 4.2 us)
Sparse Core Ops, SparseCore 0:
  10.2 24.5 all-gather.7
  38.8 50.7 all-gather.9
  91.1 16.6 all-gather.11
  109.8 40.4 all-gather.13
  151.7 25.5 all-gather.15
  210.1 72.7 reduce-scatter.5
  286.1 25.5 reduce-scatter.9
  314.3 34.6 reduce-scatter.13
  351.7 30.6 reduce-scatter.7
  384.7 51.4 reduce-scatter.11
  440.8 122.3 all-reduce.5
